TPU v7x, 32 devices: a whole 2x2x4 slice. The times are simulated.
32 devices in a mesh: ens: 2 (over y), row: 4 (over z), col: 2 (over x), chan: 2 (over core).
Axes of the slice: x: 2, y: 2, z: 4, core: 2. Of those that a mesh axis runs over, the one named last changes fastest.
Arguments:
- latent: float32 [4, 12, 32, 256], P('ens', None, 'row', 'col'), parts along dimension 0, may hold values from -6 to 6
- fresh_noise: float32 [4, 12, 32, 256], P('ens', None, 'row', 'col'), parts along dimension 0, may hold values from -6 to 6
- step_index: int32 [4], P('ens'), parts along dimension 0, may hold values from 0 to 11
- coarse: float32 [24, 4, 32], P('ens', None, 'col'), parts along dimension 0, may hold values from -6 to 6
- weight_in: bfloat16 [9, 256, 24], replicated, may hold values from -0.4375 to 0.4375
- bias_in: float32 [256], replicated, may hold values from -4 to 4
- weight_noise: float32 [256], replicated, may hold values from -4 to 4
- weight_mid: bfloat16 [9, 256, 256], P(None, 'chan'), may hold values from -0.125 to 0.125
- bias_mid: float32 [256], P('chan'), may hold values from -4 to 4
- weight_out: bfloat16 [12, 256], P(None, 'chan'), may hold values from -0.375 to 0.375
Outputs:
- fine_field: float32 [4, 12, 32, 256], P('ens', None, 'row', 'col'), parts along dimension 0
- next_latent: float32 [4, 12, 32, 256], P('ens', None, 'row', 'col'), parts along dimension 0
There are 2 independent parts, one for each index of `ens`. A program takes and returns all parts, laid end to end along the dimension named above; an argument that names none is the same for every part. Nothing has to cross between parts.
Inputs may be any that keep to these rules, and one draw needn't show every extreme that they name: `step_index`: each sample's position in the noise plan of 18 steps.
All inputs are finite; a program needn't handle non-finite values.
Results may differ from a plain program's by a relative error of at most 0.0024.
Values may be sent and summed in bfloat16 or wider, within the bound.
A program may use at most 64 MiB of HBM per device.

v0:
```python
import jax
import jax.numpy as jnp
from jax import lax
from jax.sharding import PartitionSpec as P

STEPS = 18
FACTOR = 8


sigma_data = 0.5
sigma_high = 80.0
sigma_low = 0.002
rho_power = 7.0


def extended_2(value, sides, width):
    for axis, dim in sides:
        count, length = (lax.axis_size(axis), value.shape[dim])
        up = [(i, (i + 1) % count) for i in range(count - 1)]
        down = [(j, i) for i, j in up]
        last = lax.slice_in_dim(value, length - width, length, axis=dim)
        initial = lax.slice_in_dim(value, 0, width, axis=dim)
        before = lax.ppermute(last, axis, up)
        after = lax.ppermute(initial, axis, down)
        value = jnp.concatenate([before, value, after], axis=dim)
    return value


def blend_matrix(fine_index, coarse_index, coarse_count, factor):
    twice_pos = 2 * fine_index + 1 - factor
    lower_cell = twice_pos // (2 * factor)
    fraction = (twice_pos - lower_cell * 2 * factor).astype(jnp.float32) / (2.0 * factor)
    before = lower_cell < 0
    fraction = jnp.where(before, 0.0, fraction)
    lower_clip = jnp.clip(lower_cell, 0, coarse_count - 1)
    upper_clip = jnp.clip(lower_cell + 1, 0, coarse_count - 1)
    lower_hit = (lower_clip[:, None] == coarse_index[None, :]).astype(jnp.float32)
    upper_hit = (upper_clip[:, None] == coarse_index[None, :]).astype(jnp.float32)
    return (1.0 - fraction)[:, None] * lower_hit + fraction[:, None] * upper_hit


def noise_level(position):
    top_root = sigma_high ** (1.0 / rho_power)
    bottom_root = sigma_low ** (1.0 / rho_power)
    along = position.astype(jnp.float32) / (STEPS - 1)
    return (top_root + along * (bottom_root - top_root)) ** rho_power


def conv_valid(source, weight, out_rows, out_cols):
    total = None
    for offset_row in range(3):
        for offset_col in range(3):
            window = source[
                :, :, offset_row : offset_row + out_rows, offset_col : offset_col + out_cols
            ]
            term = jnp.einsum(
                "oi,siyx->soyx",
                weight[3 * offset_row + offset_col],
                window,
                preferred_element_type=jnp.float32,
            )
            total = term if total is None else total + term
    return total


def on_device(
    latent,
    fresh_noise,
    step_index,
    coarse,
    weight_in,
    bias_in,
    weight_noise,
    weight_mid,
    bias_mid,
    weight_out,
):
    samples, channels, rows_here, cols_here = latent.shape
    row_place = lax.axis_index("row")
    col_place = lax.axis_index("col")
    height = lax.axis_size("row") * rows_here
    width = lax.axis_size("col") * cols_here
    coarse_rows = coarse.shape[1]
    local_cols = coarse.shape[2]
    coarse_cols = lax.axis_size("col") * local_cols
    widened = extended_2(coarse, (("col", 2),), 1)
    rows_matrix = blend_matrix(
        row_place * rows_here + jnp.arange(rows_here, dtype=jnp.int32),
        jnp.arange(coarse_rows, dtype=jnp.int32),
        coarse_rows,
        FACTOR,
    )
    cols_matrix = blend_matrix(
        col_place * cols_here + jnp.arange(cols_here, dtype=jnp.int32),
        col_place * local_cols - 1 + jnp.arange(local_cols + 2, dtype=jnp.int32),
        coarse_cols,
        FACTOR,
    )
    mean_up = jnp.einsum(
        "yh,khw,xw->kyx", rows_matrix, widened, cols_matrix, precision=lax.Precision.HIGHEST
    )
    noise_now = noise_level(step_index)
    noise_next = noise_level(step_index + 1)
    inputs = jnp.concatenate(
        [latent, jnp.broadcast_to(mean_up[None], (samples,) + mean_up.shape)], axis=1
    ).astype(jnp.bfloat16)
    conditioning = (
        bias_in[None, :, None, None]
        + (jnp.log(noise_now) / 4.0)[:, None, None, None] * weight_noise[None, :, None, None]
    )
    mid_full, out_full = (
        lax.all_gather(weight_mid, "chan", axis=1, tiled=True),
        lax.all_gather(weight_out, "chan", axis=1, tiled=True),
    )
    bias_full = lax.all_gather(bias_mid, "chan", axis=0, tiled=True)
    half_cols = cols_here // lax.axis_size("chan")
    chan_place = lax.axis_index("chan")
    extended = extended_2(inputs, (("row", 2), ("col", 3)), 2)
    source = lax.dynamic_slice_in_dim(extended, chan_place * half_cols, half_cols + 4, 3)
    hidden = jax.nn.silu(conv_valid(source, weight_in, rows_here + 2, half_cols + 2) + conditioning)
    global_rows = row_place * rows_here - 1 + jnp.arange(rows_here + 2, dtype=jnp.int32)
    global_cols = (
        col_place * cols_here
        + chan_place * half_cols
        - 1
        + jnp.arange(half_cols + 2, dtype=jnp.int32)
    )
    inside = ((global_rows >= 0) & (global_rows < height))[:, None] & (
        (global_cols >= 0) & (global_cols < width)
    )[None, :]
    hidden_wide = jnp.where(inside, hidden, 0.0).astype(jnp.bfloat16)
    middle = jax.nn.silu(
        conv_valid(hidden_wide, mid_full, rows_here, half_cols) + bias_full[None, :, None, None]
    ).astype(jnp.bfloat16)
    half_network = jnp.einsum("ko,soyx->skyx", out_full, middle, preferred_element_type=jnp.float32)
    network = lax.all_gather(half_network, "chan", axis=3, tiled=True)
    scale_now = jnp.sqrt(noise_now * noise_now + sigma_data * sigma_data)
    skip_coef = sigma_data * sigma_data / (noise_now * noise_now + sigma_data * sigma_data)
    out_coef = sigma_data * noise_now / scale_now
    denoised = (skip_coef * scale_now)[:, None, None, None] * latent + out_coef[
        :, None, None, None
    ] * network
    fine_field = mean_up[None] + denoised
    scale_next = jnp.sqrt(noise_next * noise_next + sigma_data * sigma_data)
    next_latent = (denoised + noise_next[:, None, None, None] * fresh_noise) / scale_next[
        :, None, None, None
    ]
    return (fine_field, next_latent)


def solution(mesh):
    in_specs = (
        P("ens", None, "row", "col"),
        P("ens", None, "row", "col"),
        P("ens"),
        P("ens", None, "col"),
        P(),
        P(),
        P(),
        P(None, "chan", None),
        P("chan"),
        P(None, "chan"),
    )
    out_specs = (P("ens", None, "row", "col"), P("ens", None, "row", "col"))
    return jax.shard_map(
        on_device, mesh=mesh, in_specs=in_specs, out_specs=out_specs, check_vma=False
    )
```

profile of v0, /device:TPU:1, one launch (start us, length us, event | category | flops | bytes accessed | tf_op | source)
XLA Modules:
  0.0 60.1 jit_solution(1089614030091482770)
XLA Ops:
  7.2 0.0 all-gather.3.cloned.1.call-start
  7.2 0.7 %copy.29 = f32[12,4,16]{2,0,1:T(8,128)S(1)} copy(f32[12,4,16]{2,1,0:T(4,128)} %param.13) | data formatting | bytes 6144 | tf_op args[3]
  8.0 0.1 fusion.95
  8.0 3.9 %collective-permute-start = (f32[12,4,1]{2,0,1:T(8,128)S(1)}, f32[12,4,1]{2,0,1:T(8,128)S(1)}, u32[]{:S(2)}, u32[]{:S(2)}) collective-permute-start(f32[12,4,1]{2,0,1:T(8,128)S(1)} %get-tuple-element.23), channel_id=1, source_target_pairs={{0,2},{1,3},{4,6},{5,7},{8,10},{9,11},{12,14},{13,15},{16,18},{17,... | collective-permute-start | bytes 584 | tf_op jit(solution)/shard_map/ppermute | solution.py:23
  12.0 1.3 %collective-permute-start.1 = (f32[12,4,1]{2,0,1:T(8,128)S(1)}, f32[12,4,1]{2,0,1:T(8,128)S(1)}, u32[]{:S(2)}, u32[]{:S(2)}) collective-permute-start(f32[12,4,1]{2,0,1:T(8,128)S(1)} %get-tuple-element.24), channel_id=1, source_target_pairs={{2,0},{3,1},{6,4},{7,5},{10,8},{11,9},{14,12},{15,13},{18,16},{19,... | collective-permute-start | bytes 584 | tf_op jit(solution)/shard_map/ppermute | solution.py:24
  13.3 0.0 all-gather.3.cloned.1.call-update
  13.5 0.8 %add_sqrt_fusion = (f32[2]{0:T(128)S(1)}, f32[2]{0:T(128)S(1)}, f32[2]{0:T(128)S(1)}, f32[2]{0:T(128)S(1)}, f32[2]{0:T(128)S(1)}) fusion(s32[2]{0:T(128)} %param.12), kind=kLoop, calls=%fused_computation.139 | loop fusion | flops 34 | bytes 48 | tf_op jit(solution)/shard_map/sqrt | solution.py:144
  14.2 0.8 %multiply_add_fusion.1 = f32[2,256]{1,0:T(2,128)S(1)} fusion(f32[256]{0:T(256)} %param.16, f32[256]{0:T(256)} %param.15, f32[2]{0:T(128)S(1)} %get-tuple-element.25), kind=kLoop, calls=%fused_computation.115 | loop fusion | flops 1024 | bytes 4104 | tf_op jit(solution)/shard_map/add | solution.py:108
  15.0 0.9 %convert.7 = bf16[2,12,8,128]{3,2,1,0:T(8,128)(2,1)S(1)} convert(f32[2,12,8,128]{3,2,1,0:T(8,128)} %param.10) | non-fusion elementwise | flops 24576 | bytes 147456 | tf_op jit(solution)/shard_map/convert
  15.9 0.8 %collective-permute-done.1 = f32[12,4,1]{2,0,1:T(8,128)S(1)} collective-permute-done((f32[12,4,1]{2,0,1:T(8,128)S(1)}, f32[12,4,1]{2,0,1:T(8,128)S(1)}, u32[]{:S(2)}, u32[]{:S(2)}) %collective-permute-start.1) | collective-permute-done | bytes 224 | tf_op jit(solution)/shard_map/ppermute | solution.py:24
  16.7 0.2 fusion.42
  16.9 0.2 fusion.96
  17.2 3.2 %collective-permute-start.2 = (bf16[2,24,2,128]{3,2,1,0:T(2,128)(2,1)S(1)}, bf16[2,24,2,128]{3,2,1,0:T(2,128)(2,1)S(1)}, u32[]{:S(2)}, u32[]{:S(2)}) collective-permute-start(bf16[2,24,2,128]{3,2,1,0:T(2,128)(2,1)S(1)} %get-tuple-element.21), channel_id=1, source_target_pairs={{0,4},{4,8},{8,12},{1,5},{5,9},{9,13},{2,6},{6,10},{10,14},{3,7},{... | collective-permute-start | bytes 73736 | tf_op jit(solution)/shard_map/ppermute | solution.py:23
  20.4 1.3 %collective-permute-start.3 = (bf16[2,24,2,128]{3,2,1,0:T(2,128)(2,1)S(1)}, bf16[2,24,2,128]{3,2,1,0:T(2,128)(2,1)S(1)}, u32[]{:S(2)}, u32[]{:S(2)}) collective-permute-start(bf16[2,24,2,128]{3,2,1,0:T(2,128)(2,1)S(1)} %get-tuple-element.22), channel_id=1, source_target_pairs={{4,0},{8,4},{12,8},{5,1},{9,5},{13,9},{6,2},{10,6},{14,10},{7,3},{... | collective-permute-start | bytes 73736 | tf_op jit(solution)/shard_map/ppermute | solution.py:24
  21.7 3.2 %collective-permute-done.3 = bf16[2,24,2,128]{3,2,1,0:T(2,128)(2,1)S(1)} collective-permute-done((bf16[2,24,2,128]{3,2,1,0:T(2,128)(2,1)S(1)}, bf16[2,24,2,128]{3,2,1,0:T(2,128)(2,1)S(1)}, u32[]{:S(2)}, u32[]{:S(2)}) %collective-permute-start.3) | collective-permute-done | bytes 24608 | tf_op jit(solution)/shard_map/ppermute | solution.py:24
  25.0 0.1 pad_maximum_fusion
  25.1 0.1 fusion.94
  25.2 3.2 %collective-permute-start.4 = (bf16[2,24,12,2]{3,2,1,0:T(8,128)(2,1)S(1)}, bf16[2,24,12,2]{3,2,1,0:T(8,128)(2,1)S(1)}, u32[]{:S(2)}, u32[]{:S(2)}) collective-permute-start(bf16[2,24,12,2]{3,2,1,0:T(8,128)(2,1)S(1)} %get-tuple-element.20), channel_id=1, source_target_pairs={{0,2},{1,3},{4,6},{5,7},{8,10},{9,11},{12,14},{13,15},{16,18},{17,... | collective-permute-start | bytes 6920 | tf_op jit(solution)/shard_map/ppermute | solution.py:23
  28.5 1.3 %collective-permute-start.5 = (bf16[2,24,12,2]{3,2,1,0:T(8,128)(2,1)S(1)}, bf16[2,24,12,2]{3,2,1,0:T(8,128)(2,1)S(1)}, u32[]{:S(2)}, u32[]{:S(2)}) collective-permute-start(bf16[2,24,12,2]{3,2,1,0:T(8,128)(2,1)S(1)} %get-tuple-element.19), channel_id=1, source_target_pairs={{2,0},{3,1},{6,4},{7,5},{10,8},{11,9},{14,12},{15,13},{18,16},{19,... | collective-permute-start | bytes 6920 | tf_op jit(solution)/shard_map/ppermute | solution.py:24
  29.8 0.1 broadcast_and_fusion
  29.8 4.4 %all-gather = f32[2,1,128]{2,1,0:T(1,128)S(1)} all-gather(f32[1,1,128]{2,1,0:T(1,128)S(1)} %bitcast.167), channel_id=1, replica_groups=mesh['ens'=2,'row'=4,'col'=2,'chan'=2] {'chan'}, dimensions={0}, use_global_device_ids=true | all-gather | bytes 1536 | tf_op jit(solution)/shard_map/all_gather | solution.py:115
  34.3 1.8 %all_gather.14 = bf16[12,256]{1,0:T(8,128)(2,1)S(1)} all-gather(bf16[12,128]{1,0:T(8,128)(2,1)S(1)} %copy-done.4), channel_id=1, replica_groups=mesh['ens'=2,'row'=4,'col'=2,'chan'=2] {'chan'}, dimensions={1}, use_global_device_ids=true | all-gather | bytes 9216 | tf_op jit(solution)/shard_map/all_gather | solution.py:113
  36.1 0.6 %fusion.21 = bf16[2,24,12,68]{3,2,1,0:T(8,128)(2,1)S(1)} fusion(s32[]{:T(128)S(6)} %select_n.69, bf16[2,24,12,2]{3,2,1,0:T(8,128)(2,1)S(1)} %collective-permute-done.4, bf16[2,24,2,128]{3,2,1,0:T(2,128)(2,1)S(1)} %collective-permute-done.2, bf16[2,12,8,128]{3,2,1,0:T(8,128)(2,1)S(1)} %convert.7, bf16[2,12,8,128]{3,2,1,0:T(8,128)(2,1)S(1)} %add.314, ...), kind=kLoop, calls=%fused_computation.39 | loop fusion | flops 470016 | bytes 230404 | tf_op jit(solution)/shard_map/concatenate | solution.py:25
  36.7 0.5 fusion.93
  37.2 0.4 copy-done.2
  37.6 0.4 fusion.26
  38.0 0.4 fusion.28
  38.4 0.4 fusion.30
  38.8 0.4 fusion.32
  39.2 0.4 fusion.34
  39.6 0.4 fusion.36
  40.0 0.4 fusion.38
  40.4 0.4 fusion.40
  40.8 1.0 %fusion.4 = bf16[2,256,10,66]{1,3,2,0:T(8,128)(2,1)S(1)} fusion(f32[2,10,66,256]{3,2,1,0:T(8,128)S(1)} %fusion.26, f32[2,10,66,256]{3,2,1,0:T(8,128)S(1)} %fusion.28, f32[2,10,66,256]{3,2,1,0:T(8,128)S(1)} %fusion.30, f32[2,10,66,256]{3,2,1,0:T(8,128)S(1)} %fusion.32, f32[2,10,66,256]{3,2,1,0:T(8,128)S(1)} %fusion.34, f32[2,10,66,256]{3,2,1,0:T(8,128)S(1)} %fusion.36, ...), kind=kOutput, calls=%fused_computation.6 | convolution fusion | flops 21288960 | bytes 12685312 | tf_op jit(solution)/shard_map/oi,siyx->soyx/dot_general | solution.py:56
  41.9 0.0 all-gather.3.cloned.1.call-done
  41.9 1.3 %fusion.16 = f32[2,8,64,256]{3,2,1,0:T(8,128)S(1)} fusion(bf16[2,256,10,66]{1,3,2,0:T(8,128)(2,1)S(1)} %fusion.4, bf16[9,256,256]{2,1,0:T(8,128)(2,1)} %all-gather.3.cloned.1.call-done), kind=kOutput, calls=%fused_computation.28 | convolution fusion | flops 134217728 | bytes 1703936 | tf_op jit(solution)/shard_map/oi,siyx->soyx/dot_general | solution.py:56
  43.3 0.3 convolution_add_fusion.7
  43.6 0.4 convolution_add_fusion.6
  44.0 0.3 convolution_add_fusion.5
  44.3 0.4 convolution_add_fusion.4
  44.7 0.3 convolution_add_fusion.3
  45.0 0.3 convolution_add_fusion.2
  45.4 0.4 convolution_add_fusion.1
  45.7 0.7 %convolution_bitcast_fusion = f32[2,12,8,64]{3,1,2,0:T(8,128)S(1)} fusion(f32[2,8,64,256]{3,2,1,0:T(8,128)S(1)} %convolution_add_fusion.1, bf16[2,256,10,66]{1,3,2,0:T(8,128)(2,1)S(1)} %fusion.4, f32[256]{0:T(256)S(1)} %bitcast.168, bf16[9,256,256]{2,1,0:T(8,128)(2,1)S(1)} %copy-done, bf16[12,256]{1,0:T(8,128)(2,1)S(1)} %all_gather.14), kind=kOutput, calls=%fused_computation.17 | convolution fusion | flops 142344192 | bytes 1762304 | tf_op jit(solution)/shard_map/ko,soyx->skyx/dot_general | solution.py:135
  46.4 0.3 copy.42
  46.8 5.2 %all_gather.15 = f32[2,12,8,128]{1,2,0,3:T(8,128)S(1)} all-gather(f32[2,12,8,64]{1,2,0,3:T(8,128)S(1)} %copy.42), channel_id=1, replica_groups=mesh['ens'=2,'row'=4,'col'=2,'chan'=2] {'chan'}, dimensions={3}, use_global_device_ids=true | all-gather | bytes 147456 | tf_op jit(solution)/shard_map/all_gather | solution.py:136
  52.0 0.4 copy.43
  52.5 0.8 %add_divide_fusion = (f32[2,12,8,128]{3,2,1,0:T(8,128)}, f32[2,12,8,128]{3,2,1,0:T(8,128)}) fusion(f32[2,12,8,128]{3,2,1,0:T(8,128)S(1)} %copy-done.3, f32[2]{0:T(128)S(1)} %get-tuple-element.6, f32[2]{0:T(128)S(1)} %get-tuple-element.7, f32[2,12,8,128]{3,2,1,0:T(8,128)S(1)} %copy.43, f32[2]{0:T(128)S(1)} %get-tuple-element.26, ...), kind=kLoop, calls=%fused_computation.70 | loop fusion | flops 172032 | bytes 540704 | tf_op jit(solution)/shard_map/div | solution.py:145
  (24 shorter events, 0.2 us)
Async XLA Ops:
  7.2 22.7 %copy-start.5 = (f32[128]{0:T(128)S(1)}, f32[128]{0:T(128)}, u32[]{:S(2)}) copy-start(f32[128]{0:T(128)} %param.18) | copy-start | bytes 1540
  7.2 27.1 %copy-start.4 = (bf16[12,128]{1,0:T(8,128)(2,1)S(1)}, bf16[12,128]{1,0:T(8,128)(2,1)}, u32[]{:S(2)}) copy-start(bf16[12,128]{1,0:T(8,128)(2,1)} %param.19) | copy-start | bytes 9220
  7.2 34.7 %all-gather.3.cloned.1.call-start = ((), (), s32[]{:S(2)}) async-start(), calls=%async_computation | async-start | bytes 1769472 | tf_op jit(solution)/shard_map/all_gather | solution.py:112
  8.0 7.8 %collective-permute-start = (f32[12,4,1]{2,0,1:T(8,128)S(1)}, f32[12,4,1]{2,0,1:T(8,128)S(1)}, u32[]{:S(2)}, u32[]{:S(2)}) collective-permute-start(f32[12,4,1]{2,0,1:T(8,128)S(1)} %get-tuple-element.23), channel_id=1, source_target_pairs={{0,2},{1,3},{4,6},{5,7},{8,10},{9,11},{12,14},{13,15},{16,18},{17,... | collective-permute-start | bytes 584 | tf_op jit(solution)/shard_map/ppermute | solution.py:23
  12.0 4.7 %collective-permute-start.1 = (f32[12,4,1]{2,0,1:T(8,128)S(1)}, f32[12,4,1]{2,0,1:T(8,128)S(1)}, u32[]{:S(2)}, u32[]{:S(2)}) collective-permute-start(f32[12,4,1]{2,0,1:T(8,128)S(1)} %get-tuple-element.24), channel_id=1, source_target_pairs={{2,0},{3,1},{6,4},{7,5},{10,8},{11,9},{14,12},{15,13},{18,16},{19,... | collective-permute-start | bytes 584 | tf_op jit(solution)/shard_map/ppermute | solution.py:24
  17.2 4.5 %collective-permute-start.2 = (bf16[2,24,2,128]{3,2,1,0:T(2,128)(2,1)S(1)}, bf16[2,24,2,128]{3,2,1,0:T(2,128)(2,1)S(1)}, u32[]{:S(2)}, u32[]{:S(2)}) collective-permute-start(bf16[2,24,2,128]{3,2,1,0:T(2,128)(2,1)S(1)} %get-tuple-element.21), channel_id=1, source_target_pairs={{0,4},{4,8},{8,12},{1,5},{5,9},{9,13},{2,6},{6,10},{10,14},{3,7},{... | collective-permute-start | bytes 73736 | tf_op jit(solution)/shard_map/ppermute | solution.py:23
  20.4 4.6 %collective-permute-start.3 = (bf16[2,24,2,128]{3,2,1,0:T(2,128)(2,1)S(1)}, bf16[2,24,2,128]{3,2,1,0:T(2,128)(2,1)S(1)}, u32[]{:S(2)}, u32[]{:S(2)}) collective-permute-start(bf16[2,24,2,128]{3,2,1,0:T(2,128)(2,1)S(1)} %get-tuple-element.22), channel_id=1, source_target_pairs={{4,0},{8,4},{12,8},{5,1},{9,5},{13,9},{6,2},{10,6},{14,10},{7,3},{... | collective-permute-start | bytes 73736 | tf_op jit(solution)/shard_map/ppermute | solution.py:24
  25.2 10.8 %collective-permute-start.4 = (bf16[2,24,12,2]{3,2,1,0:T(8,128)(2,1)S(1)}, bf16[2,24,12,2]{3,2,1,0:T(8,128)(2,1)S(1)}, u32[]{:S(2)}, u32[]{:S(2)}) collective-permute-start(bf16[2,24,12,2]{3,2,1,0:T(8,128)(2,1)S(1)} %get-tuple-element.20), channel_id=1, source_target_pairs={{0,2},{1,3},{4,6},{5,7},{8,10},{9,11},{12,14},{13,15},{16,18},{17,... | collective-permute-start | bytes 6920 | tf_op jit(solution)/shard_map/ppermute | solution.py:23
  28.5 7.6 %collective-permute-start.5 = (bf16[2,24,12,2]{3,2,1,0:T(8,128)(2,1)S(1)}, bf16[2,24,12,2]{3,2,1,0:T(8,128)(2,1)S(1)}, u32[]{:S(2)}, u32[]{:S(2)}) collective-permute-start(bf16[2,24,12,2]{3,2,1,0:T(8,128)(2,1)S(1)} %get-tuple-element.19), channel_id=1, source_target_pairs={{2,0},{3,1},{6,4},{7,5},{10,8},{11,9},{14,12},{15,13},{18,16},{19,... | collective-permute-start | bytes 6920 | tf_op jit(solution)/shard_map/ppermute | solution.py:24
  36.7 0.9 %copy-start.2 = (bf16[9,256,24]{1,2,0:T(8,128)(2,1)S(1)}, bf16[9,256,24]{1,2,0:T(8,128)(2,1)}, u32[]{:S(2)}) copy-start(bf16[9,256,24]{1,2,0:T(8,128)(2,1)} %param.14) | copy-start | bytes 331780
  41.9 1.3 %copy-start = (bf16[9,256,256]{2,1,0:T(8,128)(2,1)S(1)}, bf16[9,256,256]{2,1,0:T(8,128)(2,1)}, u32[]{:S(2)}) copy-start(bf16[9,256,256]{2,1,0:T(8,128)(2,1)} %all-gather.3.cloned.1.call-done) | copy-start | bytes 3538948
  46.8 5.7 %copy-start.1 = (f32[2,12,8,128]{3,2,1,0:T(8,128)S(1)}, f32[2,12,8,128]{3,2,1,0:T(8,128)}, u32[]{:S(2)}) copy-start(f32[2,12,8,128]{3,2,1,0:T(8,128)} %param.10) | copy-start | bytes 294916
  46.8 5.7 %copy-start.3 = (f32[2,12,8,128]{3,2,1,0:T(8,128)S(1)}, f32[2,12,8,128]{3,2,1,0:T(8,128)}, u32[]{:S(2)}) copy-start(f32[2,12,8,128]{3,2,1,0:T(8,128)} %param.11) | copy-start | bytes 294916
Sparse Core Ops, SparseCore 0:
  13.4 12.2 all-gather.2
where the time goes:
time: 60.8 us; the launch traced here: 60.1 us
  between operations  14.4 us (24%)
  starting transfers between devices  14.3 us (24%)
  blocking collectives  11.4 us (19%)
  matrix products  9.14 us (15%)
  other arithmetic  4.15 us (7%)
  waiting for transfers between devices  4.06 us (7%)
  local copies, waits for them, and re-layouts  2.63 us (4%)
    ppermute x3, starting transfers between devices, extended_2(): before = lax.ppermute(last, axis, up)  10.4 us
    dot_general x17, matrix products, conv_valid(): jnp.einsum('oi,siyx->soyx', weight[3 * offset_row + offset_col], window,...  7.96 us
    all_gather x1, blocking collectives, on_device(): network = lax.all_gather(half_network, 'chan', axis=3, tiled=True)  5.23 us
    all_gather x1, blocking collectives, on_device(): bias_full = lax.all_gather(bias_mid, 'chan', axis=0, tiled=True)  4.4 us
    ppermute x3, waiting for transfers between devices, extended_2(): after = lax.ppermute(initial, axis, down)  4.01 us
    ppermute x3, starting transfers between devices, extended_2(): after = lax.ppermute(initial, axis, down)  3.88 us
    all_gather x1, blocking collectives, on_device(): lax.all_gather(weight_out, 'chan', axis=1, tiled=True)  1.79 us
  transfers between devices with their start and end apart: 7, of which 2 were waited for; matrix products, arithmetic and copies ran while one was open for 14% of the time, Pallas kernels for 0%

commit v1 on v0

v1 whole, which is shorter than its diff:
```python
import functools

import jax
import jax.numpy as jnp
from jax import lax
from jax.experimental import pallas as pl
from jax.experimental.pallas import tpu as pltpu
from jax.sharding import PartitionSpec as P

STEPS = 18
sigma_data = 0.5
sigma_high = 80.0
sigma_low = 0.002
rho_power = 7.0
top_root = sigma_high ** (1.0 / rho_power)
bottom_root = sigma_low ** (1.0 / rho_power)

MESH = pl.DeviceIdType.MESH
UP, DOWN, LEFT, RIGHT, UL, UR, DL, DR = range(8)
STEP = {
    UP: (-1, 0), DOWN: (1, 0), LEFT: (0, -1), RIGHT: (0, 1),
    UL: (-1, -1), UR: (-1, 1), DL: (1, -1), DR: (1, 1),
}
BACK = {UP: DOWN, DOWN: UP, LEFT: RIGHT, RIGHT: LEFT, UL: DR, DR: UL, UR: DL, DL: UR}
COARSE = {LEFT: 8, RIGHT: 9}
WEIGHTS, AUX, NET, OWN = 10, 11, 12, 13
HALO = 2
GROUP = 24
BLOCK = 80
EDGE = 8


def silu(v):
    half = 0.5 * v
    return half * (1.0 + jnp.tanh(half))


def iota(shape, dim):
    return lax.broadcasted_iota(jnp.int32, shape, dim)


def blend(position, index, count, factor):
    u = (position + 0.5) / factor - 0.5
    cell = jnp.floor(u)
    fraction = jnp.where(u < 0.0, 0.0, u - cell)
    low = jnp.maximum(cell, 0.0)
    high = jnp.minimum(jnp.maximum(cell + 1.0, 0.0), count - 1.0)
    low_hit = jnp.where(low == index, 1.0 - fraction, 0.0)
    high_hit = jnp.where(high == index, fraction, 0.0)
    return low_hit + high_hit


def base_level(step):
    return top_root + step / (STEPS - 1) * (bottom_root - top_root)


def power7(b):
    b2 = b * b
    return b2 * b2 * b2 * b


def column(row_vector):
    n = row_vector.shape[1]
    parts = [
        jnp.transpose(jnp.broadcast_to(row_vector[:, a : a + 128], (128, 128)))
        for a in range(0, n, 128)
    ]
    return parts[0] if len(parts) == 1 else jnp.concatenate(parts, axis=0)


def kernel(
    sizes,
    latent_ref, fresh_ref, step_ref, coarse_ref, weight_in_ref, bias_in_ref, weight_noise_ref,
    weight_mid_ref, bias_mid_ref, weight_out_ref,
    fine_ref, next_ref,
    center, packs, coarse_t, coarse_st, aux, w_mid, w_in_t, xj, xe, hc, net, means, cond, bias_mid_col,
    send_sem, recv_sem, own_sem,
):
    n_row, n_col, factor = sizes
    samples, channels, rows, cols = latent_ref.shape
    coarse_rows, coarse_here = coarse_ref.shape[1], coarse_ref.shape[2]
    hidden = weight_in_ref.shape[2]
    half_hidden = hidden // 2
    ext = rows + 2 * HALO
    row_place, col_place = lax.axis_index("row"), lax.axis_index("col")
    me = lax.axis_index("chan")
    other = 1 - me

    def exists(d):
        dr, dc = STEP[d]
        conds = []
        if dr < 0:
            conds.append(row_place > 0)
        if dr > 0:
            conds.append(row_place < n_row - 1)
        if dc < 0:
            conds.append(col_place > 0)
        if dc > 0:
            conds.append(col_place < n_col - 1)
        return conds[0] if len(conds) == 1 else jnp.logical_and(*conds)

    def target(d):
        return {"row": row_place + STEP[d][0], "col": col_place + STEP[d][1]}

    center[...] = jnp.zeros_like(center)
    packs[...] = jnp.zeros_like(packs)
    coarse_t[...] = jnp.zeros_like(coarse_t)

    barrier = pltpu.get_barrier_semaphore()
    pl.semaphore_signal(barrier, inc=1, device_id={"chan": other}, device_id_type=MESH)
    for d in range(8):
        @pl.when(exists(d))
        def _(d=d):
            pl.semaphore_signal(barrier, inc=1, device_id=target(d), device_id_type=MESH)

    half = pl.ds(pl.multiple_of(me * half_hidden, half_hidden), half_hidden)
    own_weights = pltpu.make_async_copy(weight_mid_ref, w_mid.at[:, half, :], own_sem)
    own_weights.start()

    lane = iota((GROUP, cols), 1)
    pack = jnp.zeros((GROUP, cols), jnp.float32)
    for y in range(rows):
        center[HALO + y, 0:channels, :] = latent_ref[me, :, y, :]
        v = center[HALO + y]
        for source, place in ((cols - 1, y), (cols - 2, 16 + y), (0, cols - 1 - y), (1, cols - 17 - y)):
            pack = jnp.where(lane == place, pltpu.roll(v, (place - source) % cols, 1), pack)
    packs[8] = pack
    coarse_st[...] = jnp.zeros_like(coarse_st)
    for h in range(coarse_rows):
        start = h * GROUP + channels
        coarse_st[start : start + channels, 0:coarse_here] = coarse_ref[:, h, :]
    turned = jnp.transpose(coarse_st[...])
    coarse_t[EDGE : EDGE + coarse_here, :] = turned[0:coarse_here, :]
    aux[me] = jnp.zeros(aux.shape[1:], jnp.float32)
    aux[me, 0:channels, :] = weight_out_ref[...].astype(jnp.float32)
    aux[me, 16:17, :] = bias_mid_ref[...]

    up_ok = jnp.where(row_place > 0, 1, 0)
    down_ok = jnp.where(row_place < n_row - 1, 1, 0)
    left_ok = jnp.where(col_place > 0, 1, 0)
    right_ok = jnp.where(col_place < n_col - 1, 1, 0)
    links = (1 + up_ok + down_ok) * (1 + left_ok + right_ok)
    pl.semaphore_wait(barrier, links)

    def remote(src, dst, sem, where, arrive=None):
        return pltpu.make_async_remote_copy(
            src_ref=src, dst_ref=dst, send_sem=send_sem.at[sem],
            recv_sem=recv_sem.at[sem if arrive is None else arrive],
            device_id=where, device_id_type=MESH,
        )

    def message(d):
        arrive = BACK[d]
        if d == UP:
            src, dst = center.at[HALO : 2 * HALO], center.at[rows + HALO : rows + 2 * HALO]
        elif d == DOWN:
            src, dst = center.at[rows : rows + HALO], center.at[0:HALO]
        else:
            src, dst = packs.at[8], packs.at[arrive]
        return remote(src, dst, d, target(d), arrive)

    def coarse_message(d):
        if d == LEFT:
            src, dst = coarse_t.at[EDGE : 2 * EDGE], coarse_t.at[EDGE + coarse_here : 2 * EDGE + coarse_here]
        else:
            src, dst = coarse_t.at[coarse_here : EDGE + coarse_here], coarse_t.at[0:EDGE]
        return remote(src, dst, COARSE[d], target(d), COARSE[BACK[d]])

    for d in (LEFT, RIGHT):
        @pl.when(exists(d))
        def _(d=d):
            coarse_message(d).start()
    for d in (UL, UR, DL, DR, UP, DOWN, LEFT, RIGHT):
        @pl.when(exists(d))
        def _(d=d):
            message(d).start()
    send_aux = remote(aux.at[me], aux.at[me], AUX, {"chan": other})
    send_aux.start()
    send_weights = remote(weight_mid_ref, w_mid.at[:, half, :], WEIGHTS, {"chan": other})
    send_weights.start()

    w_in_t[...] = jnp.zeros_like(w_in_t)
    for i in range(3):
        for j in range(3):
            start = BLOCK * i + GROUP * j
            w_in_t[start : start + GROUP, :] = weight_in_ref[3 * i + j].astype(jnp.float32)
    w_first = jnp.transpose(w_in_t[...]).astype(jnp.bfloat16)[:, 0 : 3 * BLOCK]
    step_here = jnp.full((1, hidden), step_ref[me].astype(jnp.float32), jnp.float32)
    log_noise = rho_power * jnp.log(base_level(step_here))
    cond[...] = column(bias_in_ref[...] + log_noise / 4.0 * weight_noise_ref[...])

    n_coarse = coarse_t.shape[0]
    index = (iota((n_coarse, cols), 0) + (col_place * coarse_here - EDGE)).astype(jnp.float32)
    x_here = iota((n_coarse, cols), 1)
    x_edge = jnp.where(x_here < cols // 2, -2, cols - 1)
    width = n_col * cols
    tables = []
    for x in [x_here + j - 1 for j in range(3)] + [x_edge + j for j in range(3)]:
        x = x + col_place * cols
        weight = blend(x.astype(jnp.float32), index, float(n_col * coarse_here), float(factor))
        tables.append(jnp.where((x >= 0) & (x < width), weight, 0.0))
    table = jnp.concatenate(tables, axis=1)
    y_ext = iota((16, 128), 0) + (row_place * rows - HALO)
    y_valid = (y_ext >= 0) & (y_ext < n_row * rows)
    row_weights = [
        jnp.where(y_valid, blend(y_ext.astype(jnp.float32), float(h), float(coarse_rows), float(factor)), 0.0)
        for h in range(coarse_rows)
    ]

    for d in (LEFT, RIGHT):
        @pl.when(exists(d))
        def _(d=d):
            coarse_message(BACK[d]).wait_recv()
    across = lax.dot_general(
        coarse_t[...], table, (((0,), (0,)), ((), ())),
        precision=lax.Precision.HIGHEST, preferred_element_type=jnp.float32,
    )
    means[...] = across

    def mean_rows(r, which):
        total = None
        for h in range(coarse_rows):
            term = row_weights[h][r : r + 1, :] * means[h * GROUP : (h + 1) * GROUP, which * cols : (which + 1) * cols]
            total = term if total is None else total + term
        return total

    for d in (UP, DOWN, LEFT, RIGHT, UL, UR, DL, DR):
        @pl.when(exists(d))
        def _(d=d):
            message(BACK[d]).wait_recv()

    zeros = jnp.zeros((BLOCK - 3 * GROUP, cols), jnp.float32)
    for r in range(ext):
        if r < HALO:
            from_left, from_right, y = UL, UR, rows - HALO + r
        elif r < rows + HALO:
            from_left, from_right, y = LEFT, RIGHT, r - HALO
        else:
            from_left, from_right, y = DL, DR, r - rows - HALO
        pack_left, pack_right = packs[from_left], packs[from_right]
        near = jnp.where(
            lane < cols // 2, pltpu.roll(pack_left, (-y) % cols, 1), pltpu.roll(pack_right, y, 1)
        )
        far = jnp.where(
            lane < cols // 2, pltpu.roll(pack_left, (-16 - y) % cols, 1), pltpu.roll(pack_right, 16 + y, 1)
        )
        own = center[r]
        shifted = [
            jnp.where(lane == 0, near, pltpu.roll(own, 1, 1)),
            own,
            jnp.where(lane == cols - 1, near, pltpu.roll(own, cols - 1, 1)),
        ]
        edges = [
            jnp.where(lane < cols // 2, far, own),
            near,
            jnp.where(lane < cols // 2, own, far),
        ]
        here = slice(r * cols, (r + 1) * cols)
        xj[:, here] = jnp.concatenate(
            [shifted[j] + mean_rows(r, j) for j in range(3)] + [zeros], axis=0
        ).astype(jnp.bfloat16)
        xe[:, here] = jnp.concatenate(
            [edges[j] + mean_rows(r, 3 + j) for j in range(3)] + [zeros], axis=0
        ).astype(jnp.bfloat16)

    conditioning = cond[...]
    wide_lane = iota((hidden, cols), 1)
    side_ok = jnp.where(
        wide_lane < cols // 2, left_ok.astype(jnp.float32), right_ok.astype(jnp.float32)
    )
    for y in range(0, rows + 2, 2):
        def taps(ref):
            return jnp.concatenate(
                [ref[:, (y + i) * cols : (y + i + 2) * cols] for i in range(3)], axis=0
            )
        main = jnp.dot(w_first, taps(xj), preferred_element_type=jnp.float32)
        edge = jnp.dot(w_first, taps(xe), preferred_element_type=jnp.float32)
        for k in range(2):
            part = slice(k * cols, (k + 1) * cols)
            value = silu(main[:, part] + conditioning)
            side = silu(edge[:, part] + conditioning) * side_ok
            if y + k == 0:
                value, side = value * up_ok.astype(jnp.float32), side * up_ok.astype(jnp.float32)
            if y + k == rows + 1:
                value, side = value * down_ok.astype(jnp.float32), side * down_ok.astype(jnp.float32)
            before = jnp.where(wide_lane == 0, side, pltpu.roll(value, 1, 1))
            after = jnp.where(wide_lane == cols - 1, side, pltpu.roll(value, cols - 1, 1))
            here = slice((y + k) * cols, (y + k + 1) * cols)
            hc[0:hidden, here] = before.astype(jnp.bfloat16)
            hc[hidden : 2 * hidden, here] = value.astype(jnp.bfloat16)
            hc[2 * hidden : 3 * hidden, here] = after.astype(jnp.bfloat16)

    send_aux.wait_recv()
    w_out = jnp.concatenate([aux[0, 0:16], aux[1, 0:16]], axis=1).astype(jnp.bfloat16)
    bias_mid_col[...] = column(jnp.concatenate([aux[0, 16:17], aux[1, 16:17]], axis=1))
    own_weights.wait()
    send_weights.wait_recv()
    bias_wide = jnp.concatenate([bias_mid_col[...]] * 2, axis=1)
    for y in range(0, rows, 2):
        total = None
        for i in range(3):
            w = jnp.concatenate([w_mid[3 * i + j] for j in range(3)], axis=1)
            term = jnp.dot(
                w, hc[:, (y + i) * cols : (y + i + 2) * cols], preferred_element_type=jnp.float32
            )
            total = term if total is None else total + term
        middle = silu(total + bias_wide).astype(jnp.bfloat16)
        out = jnp.dot(w_out, middle, preferred_element_type=jnp.float32)
        for k in range(2):
            net[me, :, y + k, :] = out[0:channels, k * cols : (k + 1) * cols]
    send_net = remote(net.at[me], net.at[me], NET, {"chan": other})
    send_net.start()

    row_local = iota((rows, cols), 0) + row_place * rows
    out_weights = [
        blend(row_local.astype(jnp.float32), float(h), float(coarse_rows), float(factor))
        for h in range(coarse_rows)
    ]
    mean_out = []
    for c in range(channels):
        total = None
        for h in range(coarse_rows):
            at = h * GROUP + channels + c
            term = out_weights[h] * means[at : at + 1, cols : 2 * cols]
            total = term if total is None else total + term
        mean_out.append(total)

    def finish(s):
        step = jnp.full((rows, cols), step_ref[s].astype(jnp.float32), jnp.float32)
        now, later = power7(base_level(step)), power7(base_level(step + 1.0))
        variance = now * now + sigma_data * sigma_data
        scale_now = jnp.sqrt(variance)
        keep = sigma_data * sigma_data / variance * scale_now
        gain = sigma_data * now / scale_now
        shrink = 1.0 / jnp.sqrt(later * later + sigma_data * sigma_data)
        for c in range(channels):
            denoised = keep * latent_ref[s, c] + gain * net[s, c]
            fine_ref[s, c] = mean_out[c] + denoised
            next_ref[s, c] = (denoised + later * fresh_ref[s, c]) * shrink

    finish(me)
    send_net.wait_recv()
    finish(other)

    for d in range(8):
        @pl.when(exists(d))
        def _(d=d):
            message(d).wait_send()
    for d in (LEFT, RIGHT):
        @pl.when(exists(d))
        def _(d=d):
            coarse_message(d).wait_send()
    send_aux.wait_send()
    send_weights.wait_send()
    send_net.wait_send()


def on_device(
    latent, fresh_noise, step_index, coarse, weight_in, bias_in, weight_noise,
    weight_mid, bias_mid, weight_out,
):
    samples, channels, rows, cols = latent.shape
    coarse_rows, coarse_here = coarse.shape[1], coarse.shape[2]
    hidden = weight_in.shape[1]
    ext = rows + 2 * HALO
    stacked = -(-coarse_rows * GROUP // 128) * 128
    sizes = (lax.axis_size("row"), lax.axis_size("col"), cols // coarse_here)
    f32, bf16 = jnp.float32, jnp.bfloat16
    vmem = pl.BlockSpec(memory_space=pltpu.VMEM)
    specs = [vmem] * 10
    specs[2] = pl.BlockSpec(memory_space=pltpu.SMEM)
    specs[7] = pl.BlockSpec(memory_space=pl.ANY)
    return pl.pallas_call(
        functools.partial(kernel, sizes),
        out_shape=[jax.ShapeDtypeStruct(latent.shape, f32)] * 2,
        in_specs=specs,
        out_specs=[vmem, vmem],
        scratch_shapes=[
            pltpu.VMEM((ext, GROUP, cols), f32),
            pltpu.VMEM((9, GROUP, cols), f32),
            pltpu.VMEM((coarse_here + 2 * EDGE, stacked), f32),
            pltpu.VMEM((stacked, 128), f32),
            pltpu.VMEM((2, 24, hidden // 2), f32),
            pltpu.VMEM((9, hidden, hidden), bf16),
            pltpu.VMEM((256, hidden), f32),
            pltpu.VMEM((BLOCK, ext * cols), bf16),
            pltpu.VMEM((BLOCK, ext * cols), bf16),
            pltpu.VMEM((3 * hidden, (rows + 2) * cols), bf16),
            pltpu.VMEM((samples, channels, rows, cols), f32),
            pltpu.VMEM((stacked, 6 * cols), f32),
            pltpu.VMEM((hidden, cols), f32),
            pltpu.VMEM((hidden, cols), f32),
            pltpu.SemaphoreType.DMA((13,)),
            pltpu.SemaphoreType.DMA((13,)),
            pltpu.SemaphoreType.DMA,
        ],
        compiler_params=pltpu.CompilerParams(
            collective_id=0, has_side_effects=True, vmem_limit_bytes=40 * 1024 * 1024
        ),
        name="denoise_step",
    )(
        latent, fresh_noise, step_index, coarse, jnp.transpose(weight_in, (0, 2, 1)), bias_in.reshape(1, hidden),
        weight_noise.reshape(1, hidden), weight_mid, bias_mid.reshape(1, hidden // 2), weight_out,
    )


def solution(mesh):
    in_specs = (
        P("ens", None, "row", "col"),
        P("ens", None, "row", "col"),
        P("ens"),
        P("ens", None, "col"),
        P(),
        P(),
        P(),
        P(None, "chan", None),
        P("chan"),
        P(None, "chan"),
    )
    out_specs = (P("ens", None, "row", "col"), P("ens", None, "row", "col"))
    return jax.shard_map(
        on_device, mesh=mesh, in_specs=in_specs, out_specs=out_specs, check_vma=False
    )
```

time: 60.8 us -> 21.2 us (0.35)
  starting transfers between devices: 14.3 us -> 0 us
  between operations: 14.4 us -> 0.69 us
  Pallas kernels: 0 us -> 13.7 us
  blocking collectives: 11.4 us -> 0 us
  matrix products: 9.14 us -> 0 us
  other arithmetic: 4.15 us -> 0 us
  waiting for transfers between devices: 4.06 us -> 0 us
  local copies, waits for them, and re-layouts: 2.63 us -> 6.45 us
    ppermute x6 -> x0, starting transfers between devices: 14.3 us -> none  [the longest x3 10.4 us: extended_2(): before = lax.ppermute(last, axis, up)]
    pallas_call x0 -> x1, Pallas kernels: none -> 13.7 us  [on_device(): pl.pallas_call(functools.partial(kernel, sizes), out_shape=[jax.ShapeDtyp...]
    all_gather x3 -> x0, blocking collectives: 11.4 us -> none  [the longest x1 5.23 us: on_device(): network = lax.all_gather(half_network, 'chan', axis=3, tiled=True)]
    dot_general x20 -> x0, matrix products: 9.14 us -> none  [the longest x17 7.96 us: conv_valid(): jnp.einsum('oi,siyx->soyx', weight[3 * offset_row + offset_col], window,...]
    unnamed x13 -> x22, local copies, waits for them, and re-layouts: 1.2 us -> 6.45 us
    ppermute x6 -> x0, waiting for transfers between devices: 4.02 us -> none  [the longest x3 4.01 us: extended_2(): after = lax.ppermute(initial, axis, down)]
    another operation x1 -> x0, other arithmetic: 0.9 us -> none
    add x2 -> x0, other arithmetic: 0.77 us -> none  [the longest x1 0.77 us: on_device(): bias_in[None, :, None, None]]
  transfers between devices with their start and end apart: 7 -> 0, of which waited for: 2 -> 0; matrix products, arithmetic and copies ran while one was open for 14% -> 0% of each run, Pallas kernels for 0% -> 0%
where the time goes in v1:
time: 21.2 us; the launch traced here: 20.8 us
  Pallas kernels  13.7 us (65%)
  local copies, waits for them, and re-layouts  6.45 us (30%)
  between operations  0.69 us (3%)
    pallas_call x1, Pallas kernels, on_device(): pl.pallas_call(functools.partial(kernel, sizes), out_shape=[jax.ShapeDtyp...  13.7 us
    unnamed x22, local copies, waits for them, and re-layouts  6.45 us

profile of v1, /device:TPU:1, one launch (start us, length us, event | category | flops | bytes accessed | tf_op | source)
XLA Modules:
  0.0 20.8 jit_solution(12478430746524227820)
XLA Ops:
  0.6 0.0 copy-start.5
  0.6 0.0 copy-start.7
  0.7 0.0 copy-start.9
  0.7 0.0 copy-start.6
  0.7 0.0 copy-start.8
  0.7 0.6 %copy-done.5 = bf16[12,128]{1,0:T(8,128)(2,1)S(1)} copy-done((bf16[12,128]{1,0:T(8,128)(2,1)S(1)}, bf16[12,128]{1,0:T(8,128)(2,1)}, u32[]{:S(2)}) %copy-start.5) | copy-done | bytes 3096
  1.3 0.0 copy-done.7
  1.3 0.0 copy-done.9
  1.3 0.0 copy-done.6
  1.4 0.0 copy-done.8
  1.4 0.0 copy-start
  1.4 1.1 %copy-done = bf16[9,128,256]{2,1,0:T(8,128)(2,1)S(1)} copy-done((bf16[9,128,256]{2,1,0:T(8,128)(2,1)S(1)}, bf16[9,128,256]{2,1,0:T(8,128)(2,1)}, u32[]{:S(2)}) %copy-start) | copy-done | bytes 589848
  2.4 0.0 copy-start.1
  2.4 0.9 %copy-done.1 = bf16[9,256,24]{1,2,0:T(8,128)(2,1)S(1)} copy-done((bf16[9,256,24]{1,2,0:T(8,128)(2,1)S(1)}, bf16[9,256,24]{1,2,0:T(8,128)(2,1)}, u32[]{:S(2)}) %copy-start.1) | copy-done | bytes 110616
  3.3 0.0 copy-start.2
  3.3 0.9 %copy-done.2 = f32[2,12,8,128]{3,2,1,0:T(8,128)S(1)} copy-done((f32[2,12,8,128]{3,2,1,0:T(8,128)S(1)}, f32[2,12,8,128]{3,2,1,0:T(8,128)}, u32[]{:S(2)}) %copy-start.2) | copy-done | bytes 98328
  4.2 0.0 copy-start.3
  4.2 0.9 %copy-done.3 = f32[2,12,8,128]{3,2,1,0:T(8,128)S(1)} copy-done((f32[2,12,8,128]{3,2,1,0:T(8,128)S(1)}, f32[2,12,8,128]{3,2,1,0:T(8,128)}, u32[]{:S(2)}) %copy-start.3) | copy-done | bytes 98328
  5.1 0.0 copy-start.4
  5.1 0.7 %copy-done.4 = f32[12,4,16]{2,1,0:T(4,128)S(1)} copy-done((f32[12,4,16]{2,1,0:T(4,128)S(1)}, f32[12,4,16]{2,1,0:T(4,128)}, u32[]{:S(2)}) %copy-start.4) | copy-done | bytes 3096
  5.9 13.7 %denoise_step.1 = (f32[2,12,8,128]{3,2,1,0:T(8,128)S(1)}, f32[2,12,8,128]{3,2,1,0:T(8,128)S(1)}) custom-call(f32[2,12,8,128]{3,2,1,0:T(8,128)S(1)} %copy-done.2, f32[2,12,8,128]{3,2,1,0:T(8,128)S(1)} %copy-done.3, s32[2]{0:T(128)S(1)} %copy-done.8, f32[12,4,16]{2,1,0:T(4,128)S(1)} %copy-done.4, bf16[9,24,256]{2,1,0:T(8,128)(2,1)S(1)} %bitcast.4, ...), custom_call_target="tpu_custom_call" | custom-call | tf_op jit(solution)/shard_map/denoise_step/pallas_call | solution.py:373
  19.5 0.6 %copy.14 = f32[2,12,8,128]{3,2,1,0:T(8,128)} copy(f32[2,12,8,128]{3,2,1,0:T(8,128)S(1)} %get-tuple-element.4) | data formatting | bytes 196608
  20.2 0.6 %copy.15 = f32[2,12,8,128]{3,2,1,0:T(8,128)} copy(f32[2,12,8,128]{3,2,1,0:T(8,128)S(1)} %get-tuple-element.5) | data formatting | bytes 196608
Async XLA Ops:
  0.6 0.7 %copy-start.5 = (bf16[12,128]{1,0:T(8,128)(2,1)S(1)}, bf16[12,128]{1,0:T(8,128)(2,1)}, u32[]{:S(2)}) copy-start(bf16[12,128]{1,0:T(8,128)(2,1)} %weight_out_ref.1) | copy-start | bytes 9220
  0.6 0.7 %copy-start.7 = (f32[256]{0:T(256)S(1)}, f32[256]{0:T(256)}, u32[]{:S(2)}) copy-start(f32[256]{0:T(256)} %param.16) | copy-start | bytes 3076
  0.7 0.7 %copy-start.9 = (f32[128]{0:T(128)S(1)}, f32[128]{0:T(128)}, u32[]{:S(2)}) copy-start(f32[128]{0:T(128)} %param.18) | copy-start | bytes 1540
  0.7 0.7 %copy-start.6 = (f32[256]{0:T(256)S(1)}, f32[256]{0:T(256)}, u32[]{:S(2)}) copy-start(f32[256]{0:T(256)} %param.15) | copy-start | bytes 3076
  0.7 0.7 %copy-start.8 = (s32[2]{0:T(128)S(1)}, s32[2]{0:T(128)}, u32[]{:S(2)}) copy-start(s32[2]{0:T(128)} %step_ref.1) | copy-start | bytes 28
  1.4 1.1 %copy-start = (bf16[9,128,256]{2,1,0:T(8,128)(2,1)S(1)}, bf16[9,128,256]{2,1,0:T(8,128)(2,1)}, u32[]{:S(2)}) copy-start(bf16[9,128,256]{2,1,0:T(8,128)(2,1)} %weight_mid_ref.1) | copy-start | bytes 1769476
  2.4 0.9 %copy-start.1 = (bf16[9,256,24]{1,2,0:T(8,128)(2,1)S(1)}, bf16[9,256,24]{1,2,0:T(8,128)(2,1)}, u32[]{:S(2)}) copy-start(bf16[9,256,24]{1,2,0:T(8,128)(2,1)} %param.14) | copy-start | bytes 331780
  3.3 0.9 %copy-start.2 = (f32[2,12,8,128]{3,2,1,0:T(8,128)S(1)}, f32[2,12,8,128]{3,2,1,0:T(8,128)}, u32[]{:S(2)}) copy-start(f32[2,12,8,128]{3,2,1,0:T(8,128)} %latent_ref.1) | copy-start | bytes 294916
  4.2 0.9 %copy-start.3 = (f32[2,12,8,128]{3,2,1,0:T(8,128)S(1)}, f32[2,12,8,128]{3,2,1,0:T(8,128)}, u32[]{:S(2)}) copy-start(f32[2,12,8,128]{3,2,1,0:T(8,128)} %fresh_ref.1) | copy-start | bytes 294916
  5.1 0.7 %copy-start.4 = (f32[12,4,16]{2,1,0:T(4,128)S(1)}, f32[12,4,16]{2,1,0:T(4,128)}, u32[]{:S(2)}) copy-start(f32[12,4,16]{2,1,0:T(4,128)} %coarse_ref.1) | copy-start | bytes 9220

commit v2 on v1

--- a/solution.py
+++ b/solution.py
@@ -23,7 +23,7 @@
 }
 BACK = {UP: DOWN, DOWN: UP, LEFT: RIGHT, RIGHT: LEFT, UL: DR, DR: UL, UR: DL, DL: UR}
 COARSE = {LEFT: 8, RIGHT: 9}
-WEIGHTS, AUX, NET, OWN = 10, 11, 12, 13
+WEIGHTS, AUX, NET = 10, 11, 12
 HALO = 2
 GROUP = 24
 BLOCK = 80
@@ -70,9 +70,11 @@
 
 def kernel(
     sizes,
+    latent_hbm, fresh_hbm, step_hbm, coarse_hbm, weight_in_hbm, bias_in_hbm, weight_noise_hbm,
+    weight_mid_ref, bias_mid_hbm, weight_out_hbm,
+    fine_ref, next_ref,
     latent_ref, fresh_ref, step_ref, coarse_ref, weight_in_ref, bias_in_ref, weight_noise_ref,
-    weight_mid_ref, bias_mid_ref, weight_out_ref,
-    fine_ref, next_ref,
+    bias_mid_ref, weight_out_ref, load_sem,
     center, packs, coarse_t, coarse_st, aux, w_mid, w_in_t, xj, xe, hc, net, means, cond, bias_mid_col,
     send_sem, recv_sem, own_sem,
 ):
@@ -102,6 +104,17 @@
     def target(d):
         return {"row": row_place + STEP[d][0], "col": col_place + STEP[d][1]}
 
+    loads = [
+        pltpu.make_async_copy(src, dst, load_sem.at[n])
+        for n, (src, dst) in enumerate((
+            (latent_hbm, latent_ref), (coarse_hbm, coarse_ref), (weight_out_hbm, weight_out_ref),
+            (bias_mid_hbm, bias_mid_ref), (weight_in_hbm, weight_in_ref), (step_hbm, step_ref),
+            (bias_in_hbm, bias_in_ref), (weight_noise_hbm, weight_noise_ref), (fresh_hbm, fresh_ref),
+        ))
+    ]
+    for load in loads:
+        load.start()
+
     center[...] = jnp.zeros_like(center)
     packs[...] = jnp.zeros_like(packs)
     coarse_t[...] = jnp.zeros_like(coarse_t)
@@ -117,6 +130,8 @@
     own_weights = pltpu.make_async_copy(weight_mid_ref, w_mid.at[:, half, :], own_sem)
     own_weights.start()
 
+    for load in loads[0:4]:
+        load.wait()
     lane = iota((GROUP, cols), 1)
     pack = jnp.zeros((GROUP, cols), jnp.float32)
     for y in range(rows):
@@ -178,6 +193,9 @@
     send_aux.start()
     send_weights = remote(weight_mid_ref, w_mid.at[:, half, :], WEIGHTS, {"chan": other})
     send_weights.start()
+
+    for load in loads[4:]:
+        load.wait()
 
     w_in_t[...] = jnp.zeros_like(w_in_t)
     for i in range(3):
@@ -263,12 +281,18 @@
             [edges[j] + mean_rows(r, 3 + j) for j in range(3)] + [zeros], axis=0
         ).astype(jnp.bfloat16)
 
-    conditioning = cond[...]
+    send_aux.wait_recv()
+    w_out = jnp.concatenate([aux[0, 0:16], aux[1, 0:16]], axis=1).astype(jnp.bfloat16)
+    bias_mid_col[...] = column(jnp.concatenate([aux[0, 16:17], aux[1, 16:17]], axis=1))
+    own_weights.wait()
+    send_weights.wait_recv()
+
     wide_lane = iota((hidden, cols), 1)
     side_ok = jnp.where(
-        wide_lane < cols // 2, left_ok.astype(jnp.float32), right_ok.astype(jnp.float32)
+        iota((1, cols), 1) < cols // 2, left_ok.astype(jnp.float32), right_ok.astype(jnp.float32)
     )
-    for y in range(0, rows + 2, 2):
+
+    def first_section(y):
         def taps(ref):
             return jnp.concatenate(
                 [ref[:, (y + i) * cols : (y + i + 2) * cols] for i in range(3)], axis=0
@@ -277,8 +301,8 @@
         edge = jnp.dot(w_first, taps(xe), preferred_element_type=jnp.float32)
         for k in range(2):
             part = slice(k * cols, (k + 1) * cols)
-            value = silu(main[:, part] + conditioning)
-            side = silu(edge[:, part] + conditioning) * side_ok
+            value = silu(main[:, part] + cond[...])
+            side = silu(edge[:, part] + cond[...]) * side_ok
             if y + k == 0:
                 value, side = value * up_ok.astype(jnp.float32), side * up_ok.astype(jnp.float32)
             if y + k == rows + 1:
@@ -290,13 +314,11 @@
             hc[hidden : 2 * hidden, here] = value.astype(jnp.bfloat16)
             hc[2 * hidden : 3 * hidden, here] = after.astype(jnp.bfloat16)
 
-    send_aux.wait_recv()
-    w_out = jnp.concatenate([aux[0, 0:16], aux[1, 0:16]], axis=1).astype(jnp.bfloat16)
-    bias_mid_col[...] = column(jnp.concatenate([aux[0, 16:17], aux[1, 16:17]], axis=1))
-    own_weights.wait()
-    send_weights.wait_recv()
-    bias_wide = jnp.concatenate([bias_mid_col[...]] * 2, axis=1)
-    for y in range(0, rows, 2):
+    def net_message(p):
+        part = net.at[me, 2 * p : 2 * p + 2]
+        return remote(part, part, NET + p, {"chan": other})
+
+    def second_section(y):
         total = None
         for i in range(3):
             w = jnp.concatenate([w_mid[3 * i + j] for j in range(3)], axis=1)
@@ -304,12 +326,20 @@
                 w, hc[:, (y + i) * cols : (y + i + 2) * cols], preferred_element_type=jnp.float32
             )
             total = term if total is None else total + term
-        middle = silu(total + bias_wide).astype(jnp.bfloat16)
+        wide = jnp.concatenate([bias_mid_col[...]] * 2, axis=1)
+        middle = silu(total + wide).astype(jnp.bfloat16)
         out = jnp.dot(w_out, middle, preferred_element_type=jnp.float32)
         for k in range(2):
-            net[me, :, y + k, :] = out[0:channels, k * cols : (k + 1) * cols]
-    send_net = remote(net.at[me], net.at[me], NET, {"chan": other})
-    send_net.start()
+            net[me, y + k] = out[:, k * cols : (k + 1) * cols]
+
+    first_section(0)
+    first_section(2)
+    for y in range(0, rows, 2):
+        second_section(y)
+        if y + 4 < rows + 2:
+            first_section(y + 4)
+    for p in range(rows // 2):
+        net_message(p).start()
 
     row_local = iota((rows, cols), 0) + row_place * rows
     out_weights = [
@@ -334,12 +364,13 @@
         gain = sigma_data * now / scale_now
         shrink = 1.0 / jnp.sqrt(later * later + sigma_data * sigma_data)
         for c in range(channels):
-            denoised = keep * latent_ref[s, c] + gain * net[s, c]
+            denoised = keep * latent_ref[s, c] + gain * net[s, :, c, :]
             fine_ref[s, c] = mean_out[c] + denoised
             next_ref[s, c] = (denoised + later * fresh_ref[s, c]) * shrink
 
     finish(me)
-    send_net.wait_recv()
+    for p in range(rows // 2):
+        net_message(p).wait_recv()
     finish(other)
 
     for d in range(8):
@@ -352,7 +383,8 @@
             coarse_message(d).wait_send()
     send_aux.wait_send()
     send_weights.wait_send()
-    send_net.wait_send()
+    for p in range(rows // 2):
+        net_message(p).wait_send()
 
 
 def on_device(
@@ -367,15 +399,23 @@
     sizes = (lax.axis_size("row"), lax.axis_size("col"), cols // coarse_here)
     f32, bf16 = jnp.float32, jnp.bfloat16
     vmem = pl.BlockSpec(memory_space=pltpu.VMEM)
-    specs = [vmem] * 10
-    specs[2] = pl.BlockSpec(memory_space=pltpu.SMEM)
-    specs[7] = pl.BlockSpec(memory_space=pl.ANY)
+    specs = [pl.BlockSpec(memory_space=pltpu.HBM)] * 10
     return pl.pallas_call(
         functools.partial(kernel, sizes),
         out_shape=[jax.ShapeDtypeStruct(latent.shape, f32)] * 2,
         in_specs=specs,
         out_specs=[vmem, vmem],
         scratch_shapes=[
+            pltpu.VMEM(latent.shape, f32),
+            pltpu.VMEM(latent.shape, f32),
+            pltpu.SMEM(step_index.shape, jnp.int32),
+            pltpu.VMEM(coarse.shape, f32),
+            pltpu.VMEM((9, weight_in.shape[2], hidden), bf16),
+            pltpu.VMEM((1, hidden), f32),
+            pltpu.VMEM((1, hidden), f32),
+            pltpu.VMEM((1, hidden // 2), f32),
+            pltpu.VMEM(weight_out.shape, bf16),
+            pltpu.SemaphoreType.DMA((9,)),
             pltpu.VMEM((ext, GROUP, cols), f32),
             pltpu.VMEM((9, GROUP, cols), f32),
             pltpu.VMEM((coarse_here + 2 * EDGE, stacked), f32),
@@ -386,16 +426,16 @@
             pltpu.VMEM((BLOCK, ext * cols), bf16),
             pltpu.VMEM((BLOCK, ext * cols), bf16),
             pltpu.VMEM((3 * hidden, (rows + 2) * cols), bf16),
-            pltpu.VMEM((samples, channels, rows, cols), f32),
+            pltpu.VMEM((samples, rows, 16, cols), f32),
             pltpu.VMEM((stacked, 6 * cols), f32),
             pltpu.VMEM((hidden, cols), f32),
             pltpu.VMEM((hidden, cols), f32),
-            pltpu.SemaphoreType.DMA((13,)),
-            pltpu.SemaphoreType.DMA((13,)),
+            pltpu.SemaphoreType.DMA((12 + rows // 2,)),
+            pltpu.SemaphoreType.DMA((12 + rows // 2,)),
             pltpu.SemaphoreType.DMA,
         ],
         compiler_params=pltpu.CompilerParams(
-            collective_id=0, has_side_effects=True, vmem_limit_bytes=40 * 1024 * 1024
+            collective_id=0, has_side_effects=True, vmem_limit_bytes=64 * 1024 * 1024
         ),
         name="denoise_step",
     )(

time: 21.2 us -> 17.5 us (0.83)
  local copies, waits for them, and re-layouts: 6.45 us -> 2.22 us
  Pallas kernels: 13.7 us -> 14.4 us
    unnamed x22 -> x4, local copies, waits for them, and re-layouts: 6.45 us -> 2.22 us
    pallas_call x1, Pallas kernels: 13.7 us -> 14.4 us  [on_device(): pl.pallas_call(functools.partial(kernel, sizes), out_shape=[jax.ShapeDtyp...]
where the time goes in v2:
time: 17.5 us; the launch traced here: 17.3 us
  Pallas kernels  14.4 us (82%)
  local copies, waits for them, and re-layouts  2.22 us (13%)
  between operations  0.65 us (4%)
    pallas_call x1, Pallas kernels, on_device(): pl.pallas_call(functools.partial(kernel, sizes), out_shape=[jax.ShapeDtyp...  14.4 us
    unnamed x4, local copies, waits for them, and re-layouts  2.22 us

profile of v2, /device:TPU:1, one launch (start us, length us, event | category | flops | bytes accessed | tf_op | source)
XLA Modules:
  0.0 17.3 jit_solution(9450707122665383329)
XLA Ops:
  0.6 14.4 %denoise_step.1 = (f32[2,12,8,128]{3,2,1,0:T(8,128)}, f32[2,12,8,128]{3,2,1,0:T(8,128)}) custom-call(f32[2,12,8,128]{3,2,1,0:T(8,128)} %latent_hbm.1, f32[2,12,8,128]{3,2,1,0:T(8,128)} %fresh_hbm.1, s32[2]{0:T(128)} %step_hbm.1, f32[12,4,16]{2,1,0:T(4,128)} %coarse_hbm.1, bf16[9,24,256]{2,1,0:T(8,128)(2,1)} %bitcast.4, f32[1,256]{1,0:T(1,128)} %bitcast.5, ...), custom_call_target="tpu_custom_call" | custom-call | tf_op jit(solution)/shard_map/denoise_step/pallas_call | solution.py:403
  15.1 0.0 copy-start
  15.1 1.6 %copy.14 = f32[2,12,8,128]{3,2,1,0:T(8,128)} copy(f32[2,12,8,128]{3,2,1,0:T(8,128)} %get-tuple-element.4) | data formatting | bytes 196608
  16.6 0.0 copy-done
  16.6 0.6 %copy.15 = f32[2,12,8,128]{3,2,1,0:T(8,128)} copy(f32[2,12,8,128]{3,2,1,0:T(8,128)S(1)} %copy-done) | data formatting | bytes 196608
Async XLA Ops:
  15.1 1.6 %copy-start = (f32[2,12,8,128]{3,2,1,0:T(8,128)S(1)}, f32[2,12,8,128]{3,2,1,0:T(8,128)}, u32[]{:S(2)}) copy-start(f32[2,12,8,128]{3,2,1,0:T(8,128)} %get-tuple-element.5) | copy-start | bytes 294916

commit v3 on v2

--- a/solution.py
+++ b/solution.py
@@ -72,7 +72,8 @@
     sizes,
     latent_hbm, fresh_hbm, step_hbm, coarse_hbm, weight_in_hbm, bias_in_hbm, weight_noise_hbm,
     weight_mid_ref, bias_mid_hbm, weight_out_hbm,
-    fine_ref, next_ref,
+    denoised_hbm, mean_hbm, noise_hbm, shrink_hbm,
+    denoised_ref, mean_ref, noise_ref, shrink_ref, store_sem,
     latent_ref, fresh_ref, step_ref, coarse_ref, weight_in_ref, bias_in_ref, weight_noise_ref,
     bias_mid_ref, weight_out_ref, load_sem,
     center, packs, coarse_t, coarse_st, aux, w_mid, w_in_t, xj, xe, hc, net, means, cond, bias_mid_col,
@@ -130,12 +131,53 @@
     own_weights = pltpu.make_async_copy(weight_mid_ref, w_mid.at[:, half, :], own_sem)
     own_weights.start()
 
-    for load in loads[0:4]:
+    up_ok = jnp.where(row_place > 0, 1, 0)
+    down_ok = jnp.where(row_place < n_row - 1, 1, 0)
+    left_ok = jnp.where(col_place > 0, 1, 0)
+    right_ok = jnp.where(col_place < n_col - 1, 1, 0)
+    pl.semaphore_wait(barrier, (1 + up_ok + down_ok) * (1 + left_ok + right_ok))
+
+    def remote(src, dst, sem, where, arrive=None):
+        return pltpu.make_async_remote_copy(
+            src_ref=src, dst_ref=dst, send_sem=send_sem.at[sem],
+            recv_sem=recv_sem.at[sem if arrive is None else arrive],
+            device_id=where, device_id_type=MESH,
+        )
+
+    def message(d):
+        arrive = BACK[d]
+        if d == UP:
+            src, dst = center.at[HALO : 2 * HALO], center.at[rows + HALO : rows + 2 * HALO]
+        elif d == DOWN:
+            src, dst = center.at[rows : rows + HALO], center.at[0:HALO]
+        else:
+            src, dst = packs.at[8], packs.at[arrive]
+        return remote(src, dst, d, target(d), arrive)
+
+    def coarse_message(d):
+        if d == LEFT:
+            src, dst = coarse_t.at[EDGE : 2 * EDGE], coarse_t.at[EDGE + coarse_here : 2 * EDGE + coarse_here]
+        else:
+            src, dst = coarse_t.at[coarse_here : EDGE + coarse_here], coarse_t.at[0:EDGE]
+        return remote(src, dst, COARSE[d], target(d), COARSE[BACK[d]])
+
+    def each(directions, act):
+        for d in directions:
+            @pl.when(exists(d))
+            def _(d=d):
+                act(d)
+
+    send_weights = remote(weight_mid_ref, w_mid.at[:, half, :], WEIGHTS, {"chan": other})
+    send_weights.start()
+
+    for load in loads[0:2]:
         load.wait()
     lane = iota((GROUP, cols), 1)
+    for y in range(rows):
+        center[HALO + y, 0:channels, :] = latent_ref[me, :, y, :]
+    each((UP, DOWN), lambda d: message(d).start())
     pack = jnp.zeros((GROUP, cols), jnp.float32)
     for y in range(rows):
-        center[HALO + y, 0:channels, :] = latent_ref[me, :, y, :]
         v = center[HALO + y]
         for source, place in ((cols - 1, y), (cols - 2, 16 + y), (0, cols - 1 - y), (1, cols - 17 - y)):
             pack = jnp.where(lane == place, pltpu.roll(v, (place - source) % cols, 1), pack)
@@ -146,54 +188,15 @@
         coarse_st[start : start + channels, 0:coarse_here] = coarse_ref[:, h, :]
     turned = jnp.transpose(coarse_st[...])
     coarse_t[EDGE : EDGE + coarse_here, :] = turned[0:coarse_here, :]
+    each((UL, UR, DL, DR, LEFT, RIGHT), lambda d: message(d).start())
+    each((LEFT, RIGHT), lambda d: coarse_message(d).start())
+    for load in loads[2:4]:
+        load.wait()
     aux[me] = jnp.zeros(aux.shape[1:], jnp.float32)
     aux[me, 0:channels, :] = weight_out_ref[...].astype(jnp.float32)
     aux[me, 16:17, :] = bias_mid_ref[...]
-
-    up_ok = jnp.where(row_place > 0, 1, 0)
-    down_ok = jnp.where(row_place < n_row - 1, 1, 0)
-    left_ok = jnp.where(col_place > 0, 1, 0)
-    right_ok = jnp.where(col_place < n_col - 1, 1, 0)
-    links = (1 + up_ok + down_ok) * (1 + left_ok + right_ok)
-    pl.semaphore_wait(barrier, links)
-
-    def remote(src, dst, sem, where, arrive=None):
-        return pltpu.make_async_remote_copy(
-            src_ref=src, dst_ref=dst, send_sem=send_sem.at[sem],
-            recv_sem=recv_sem.at[sem if arrive is None else arrive],
-            device_id=where, device_id_type=MESH,
-        )
-
-    def message(d):
-        arrive = BACK[d]
-        if d == UP:
-            src, dst = center.at[HALO : 2 * HALO], center.at[rows + HALO : rows + 2 * HALO]
-        elif d == DOWN:
-            src, dst = center.at[rows : rows + HALO], center.at[0:HALO]
-        else:
-            src, dst = packs.at[8], packs.at[arrive]
-        return remote(src, dst, d, target(d), arrive)
-
-    def coarse_message(d):
-        if d == LEFT:
-            src, dst = coarse_t.at[EDGE : 2 * EDGE], coarse_t.at[EDGE + coarse_here : 2 * EDGE + coarse_here]
-        else:
-            src, dst = coarse_t.at[coarse_here : EDGE + coarse_here], coarse_t.at[0:EDGE]
-        return remote(src, dst, COARSE[d], target(d), COARSE[BACK[d]])
-
-    for d in (LEFT, RIGHT):
-        @pl.when(exists(d))
-        def _(d=d):
-            coarse_message(d).start()
-    for d in (UL, UR, DL, DR, UP, DOWN, LEFT, RIGHT):
-        @pl.when(exists(d))
-        def _(d=d):
-            message(d).start()
     send_aux = remote(aux.at[me], aux.at[me], AUX, {"chan": other})
     send_aux.start()
-    send_weights = remote(weight_mid_ref, w_mid.at[:, half, :], WEIGHTS, {"chan": other})
-    send_weights.start()
-
     for load in loads[4:]:
         load.wait()
 
@@ -225,10 +228,7 @@
         for h in range(coarse_rows)
     ]
 
-    for d in (LEFT, RIGHT):
-        @pl.when(exists(d))
-        def _(d=d):
-            coarse_message(BACK[d]).wait_recv()
+    each((LEFT, RIGHT), lambda d: coarse_message(BACK[d]).wait_recv())
     across = lax.dot_general(
         coarse_t[...], table, (((0,), (0,)), ((), ())),
         precision=lax.Precision.HIGHEST, preferred_element_type=jnp.float32,
@@ -242,13 +242,42 @@
             total = term if total is None else total + term
         return total
 
-    for d in (UP, DOWN, LEFT, RIGHT, UL, UR, DL, DR):
-        @pl.when(exists(d))
-        def _(d=d):
-            message(BACK[d]).wait_recv()
+    row_local = iota((rows, cols), 0) + row_place * rows
+    out_weights = [
+        blend(row_local.astype(jnp.float32), float(h), float(coarse_rows), float(factor))
+        for h in range(coarse_rows)
+    ]
+    for c in range(channels):
+        total = None
+        for h in range(coarse_rows):
+            at = h * GROUP + channels + c
+            term = out_weights[h] * means[at : at + 1, cols : 2 * cols]
+            total = term if total is None else total + term
+        mean_ref[c] = total
+
+    def levels(s):
+        step = jnp.full((rows, cols), step_ref[s].astype(jnp.float32), jnp.float32)
+        return power7(base_level(step)), power7(base_level(step + 1.0))
+
+    for s in range(samples):
+        now, later = levels(s)
+        shrink = 1.0 / jnp.sqrt(later * later + sigma_data * sigma_data)
+        shrink_ref[s, 0] = shrink
+        for c in range(channels):
+            noise_ref[s, c] = later * fresh_ref[s, c] * shrink
+    stores = [
+        pltpu.make_async_copy(src, dst, store_sem.at[n])
+        for n, (src, dst) in enumerate((
+            (mean_ref, mean_hbm), (noise_ref, noise_hbm), (shrink_ref, shrink_hbm),
+            (denoised_ref.at[me], denoised_hbm.at[me]), (denoised_ref.at[other], denoised_hbm.at[other]),
+        ))
+    ]
+    for store in stores[0:3]:
+        store.start()
 
     zeros = jnp.zeros((BLOCK - 3 * GROUP, cols), jnp.float32)
-    for r in range(ext):
+
+    def prepare(r):
         if r < HALO:
             from_left, from_right, y = UL, UR, rows - HALO + r
         elif r < rows + HALO:
@@ -281,12 +310,6 @@
             [edges[j] + mean_rows(r, 3 + j) for j in range(3)] + [zeros], axis=0
         ).astype(jnp.bfloat16)
 
-    send_aux.wait_recv()
-    w_out = jnp.concatenate([aux[0, 0:16], aux[1, 0:16]], axis=1).astype(jnp.bfloat16)
-    bias_mid_col[...] = column(jnp.concatenate([aux[0, 16:17], aux[1, 16:17]], axis=1))
-    own_weights.wait()
-    send_weights.wait_recv()
-
     wide_lane = iota((hidden, cols), 1)
     side_ok = jnp.where(
         iota((1, cols), 1) < cols // 2, left_ok.astype(jnp.float32), right_ok.astype(jnp.float32)
@@ -332,46 +355,46 @@
         for k in range(2):
             net[me, y + k] = out[:, k * cols : (k + 1) * cols]
 
+    each((LEFT, RIGHT), lambda d: message(BACK[d]).wait_recv())
+    for r in range(HALO, rows + HALO):
+        prepare(r)
+    send_aux.wait_recv()
+    w_out = jnp.concatenate([aux[0, 0:16], aux[1, 0:16]], axis=1).astype(jnp.bfloat16)
+    bias_mid_col[...] = column(jnp.concatenate([aux[0, 16:17], aux[1, 16:17]], axis=1))
+    own_weights.wait()
+    send_weights.wait_recv()
+
+    first_section(2)
+    for y in range(2, rows - 2, 2):
+        first_section(y + 2)
+        second_section(y)
+    for p in range(1, rows // 2 - 1):
+        net_message(p).start()
+    each((UP, DOWN, UL, UR, DL, DR), lambda d: message(BACK[d]).wait_recv())
+    for r in [*range(HALO), *range(rows + HALO, ext)]:
+        prepare(r)
     first_section(0)
-    first_section(2)
-    for y in range(0, rows, 2):
-        second_section(y)
-        if y + 4 < rows + 2:
-            first_section(y + 4)
-    for p in range(rows // 2):
+    first_section(rows)
+    second_section(0)
+    second_section(rows - 2)
+    for p in (0, rows // 2 - 1):
         net_message(p).start()
 
-    row_local = iota((rows, cols), 0) + row_place * rows
-    out_weights = [
-        blend(row_local.astype(jnp.float32), float(h), float(coarse_rows), float(factor))
-        for h in range(coarse_rows)
-    ]
-    mean_out = []
-    for c in range(channels):
-        total = None
-        for h in range(coarse_rows):
-            at = h * GROUP + channels + c
-            term = out_weights[h] * means[at : at + 1, cols : 2 * cols]
-            total = term if total is None else total + term
-        mean_out.append(total)
-
     def finish(s):
-        step = jnp.full((rows, cols), step_ref[s].astype(jnp.float32), jnp.float32)
-        now, later = power7(base_level(step)), power7(base_level(step + 1.0))
+        now, later = levels(s)
         variance = now * now + sigma_data * sigma_data
         scale_now = jnp.sqrt(variance)
         keep = sigma_data * sigma_data / variance * scale_now
         gain = sigma_data * now / scale_now
-        shrink = 1.0 / jnp.sqrt(later * later + sigma_data * sigma_data)
         for c in range(channels):
-            denoised = keep * latent_ref[s, c] + gain * net[s, :, c, :]
-            fine_ref[s, c] = mean_out[c] + denoised
-            next_ref[s, c] = (denoised + later * fresh_ref[s, c]) * shrink
+            denoised_ref[s, c] = keep * latent_ref[s, c] + gain * net[s, :, c, :]
 
     finish(me)
+    stores[3].start()
     for p in range(rows // 2):
         net_message(p).wait_recv()
     finish(other)
+    stores[4].start()
 
     for d in range(8):
         @pl.when(exists(d))
@@ -385,6 +408,8 @@
     send_weights.wait_send()
     for p in range(rows // 2):
         net_message(p).wait_send()
+    for store in stores:
+        store.wait()
 
 
 def on_device(
@@ -398,14 +423,16 @@
     stacked = -(-coarse_rows * GROUP // 128) * 128
     sizes = (lax.axis_size("row"), lax.axis_size("col"), cols // coarse_here)
     f32, bf16 = jnp.float32, jnp.bfloat16
-    vmem = pl.BlockSpec(memory_space=pltpu.VMEM)
     specs = [pl.BlockSpec(memory_space=pltpu.HBM)] * 10
-    return pl.pallas_call(
+    out_shapes = [latent.shape, latent.shape[1:], latent.shape, (samples, 1, rows, cols)]
+    denoised, mean, noise, shrink = pl.pallas_call(
         functools.partial(kernel, sizes),
-        out_shape=[jax.ShapeDtypeStruct(latent.shape, f32)] * 2,
+        out_shape=[jax.ShapeDtypeStruct(shape, f32) for shape in out_shapes],
         in_specs=specs,
-        out_specs=[vmem, vmem],
+        out_specs=[pl.BlockSpec(memory_space=pltpu.HBM)] * 4,
         scratch_shapes=[
+            *[pltpu.VMEM(shape, f32) for shape in out_shapes],
+            pltpu.SemaphoreType.DMA((5,)),
             pltpu.VMEM(latent.shape, f32),
             pltpu.VMEM(latent.shape, f32),
             pltpu.SMEM(step_index.shape, jnp.int32),
@@ -442,6 +469,7 @@
         latent, fresh_noise, step_index, coarse, jnp.transpose(weight_in, (0, 2, 1)), bias_in.reshape(1, hidden),
         weight_noise.reshape(1, hidden), weight_mid, bias_mid.reshape(1, hidden // 2), weight_out,
     )
+    return mean[None] + denoised, denoised * shrink + noise
 
 
 def solution(mesh):

time: 17.5 us -> 17.1 us (0.977)
  other arithmetic: 0 us -> 1.63 us
  local copies, waits for them, and re-layouts: 2.22 us -> 0.69 us
  Pallas kernels: 14.4 us -> 13.9 us
    add x0 -> x1, other arithmetic: none -> 1.63 us  [on_device(): return (mean[None] + denoised, denoised * shrink + noise)]
    unnamed x4 -> x2, local copies, waits for them, and re-layouts: 2.22 us -> 0.69 us
    pallas_call x1, Pallas kernels: 14.4 us -> 13.9 us  [on_device(): pl.pallas_call(functools.partial(kernel, sizes), out_shape=[jax.ShapeDtyp...]
where the time goes in v3:
time: 17.1 us; the launch traced here: 16.9 us
  Pallas kernels  13.9 us (81%)
  other arithmetic  1.63 us (10%)
  local copies, waits for them, and re-layouts  0.69 us (4%)
  between operations  0.65 us (4%)
    pallas_call x1, Pallas kernels, on_device(): pl.pallas_call(functools.partial(kernel, sizes), out_shape=[jax.ShapeDtyp...  13.9 us
    add x1, other arithmetic, on_device(): return (mean[None] + denoised, denoised * shrink + noise)  1.63 us
    unnamed x2, local copies, waits for them, and re-layouts  0.69 us

profile of v3, /device:TPU:1, one launch (start us, length us, event | category | flops | bytes accessed | tf_op | source)
XLA Modules:
  0.0 16.9 jit_solution(10474356354707288544)
XLA Ops:
  0.6 13.9 %denoise_step.1 = (f32[2,12,8,128]{3,2,1,0:T(8,128)}, f32[12,8,128]{2,1,0:T(8,128)}, f32[2,12,8,128]{3,2,1,0:T(8,128)}, f32[2,1,8,128]{3,2,1,0:T(8,128)}) custom-call(f32[2,12,8,128]{3,2,1,0:T(8,128)} %latent_hbm.1, f32[2,12,8,128]{3,2,1,0:T(8,128)} %fresh_hbm.1, s32[2]{0:T(128)} %step_hbm.1, f32[12,4,16]{2,1,0:T(4,128)} %coarse_hbm.1, ...), custom_call_target="tpu_custom_call" | custom-call | tf_op jit(solution)/shard_map/denoise_step/pallas_call | solution.py:428
  14.5 0.0 copy-start
  14.5 0.7 %copy-done = f32[2,1,8,128]{3,2,1,0:T(8,128)S(1)} copy-done((f32[2,1,8,128]{3,2,1,0:T(8,128)S(1)}, f32[2,1,8,128]{3,2,1,0:T(8,128)}, u32[]{:S(2)}) %copy-start) | copy-done | bytes 8216
  15.2 1.6 %multiply_add_fusion = (f32[2,12,8,128]{3,2,1,0:T(8,128)}, f32[2,12,8,128]{3,2,1,0:T(8,128)}) fusion(f32[2,12,8,128]{3,2,1,0:T(8,128)} %get-tuple-element.9, f32[2,12,8,128]{3,2,1,0:T(8,128)} %get-tuple-element.7, f32[2,8,128]{2,1,0:T(8,128)S(1)} %bitcast.6, f32[12,8,128]{2,1,0:T(8,128)} %get-tuple-element.6), kind=kLoop, calls=%fused_computation | loop fusion | flops 73728 | bytes 450560 | tf_op jit(solution)/shard_map/add | solution.py:472
Async XLA Ops:
  14.5 0.7 %copy-start = (f32[2,1,8,128]{3,2,1,0:T(8,128)S(1)}, f32[2,1,8,128]{3,2,1,0:T(8,128)}, u32[]{:S(2)}) copy-start(f32[2,1,8,128]{3,2,1,0:T(8,128)} %get-tuple-element.8) | copy-start | bytes 24580

commit v4 on v3

--- a/solution.py
+++ b/solution.py
@@ -262,9 +262,9 @@
     for s in range(samples):
         now, later = levels(s)
         shrink = 1.0 / jnp.sqrt(later * later + sigma_data * sigma_data)
-        shrink_ref[s, 0] = shrink
         for c in range(channels):
             noise_ref[s, c] = later * fresh_ref[s, c] * shrink
+            shrink_ref[s, c] = shrink
     stores = [
         pltpu.make_async_copy(src, dst, store_sem.at[n])
         for n, (src, dst) in enumerate((
@@ -424,7 +424,7 @@
     sizes = (lax.axis_size("row"), lax.axis_size("col"), cols // coarse_here)
     f32, bf16 = jnp.float32, jnp.bfloat16
     specs = [pl.BlockSpec(memory_space=pltpu.HBM)] * 10
-    out_shapes = [latent.shape, latent.shape[1:], latent.shape, (samples, 1, rows, cols)]
+    out_shapes = [latent.shape, latent.shape[1:], latent.shape, latent.shape]
     denoised, mean, noise, shrink = pl.pallas_call(
         functools.partial(kernel, sizes),
         out_shape=[jax.ShapeDtypeStruct(shape, f32) for shape in out_shapes],

time: 17.1 us -> 16.4 us (0.959)
  local copies, waits for them, and re-layouts: 0.69 us -> 0 us
    unnamed x2 -> x0, local copies, waits for them, and re-layouts: 0.69 us -> none
where the time goes in v4:
time: 16.4 us; the launch traced here: 16.2 us
  Pallas kernels  13.9 us (85%)
  other arithmetic  1.69 us (10%)
  between operations  0.64 us (4%)
    pallas_call x1, Pallas kernels, on_device(): pl.pallas_call(functools.partial(kernel, sizes), out_shape=[jax.ShapeDtyp...  13.9 us
    add x1, other arithmetic, on_device(): return (mean[None] + denoised, denoised * shrink + noise)  1.69 us

profile of v4, /device:TPU:1, one launch (start us, length us, event | category | flops | bytes accessed | tf_op | source)
XLA Modules:
  0.0 16.2 jit_solution(6554381181879418058)
XLA Ops:
  0.6 13.9 %denoise_step.1 = (f32[2,12,8,128]{3,2,1,0:T(8,128)}, f32[12,8,128]{2,1,0:T(8,128)}, f32[2,12,8,128]{3,2,1,0:T(8,128)}, f32[2,12,8,128]{3,2,1,0:T(8,128)}) custom-call(f32[2,12,8,128]{3,2,1,0:T(8,128)} %latent_hbm.1, f32[2,12,8,128]{3,2,1,0:T(8,128)} %fresh_hbm.1, s32[2]{0:T(128)} %step_hbm.1, f32[12,4,16]{2,1,0:T(4,128)} %coarse_hbm.1, ...), custom_call_target="tpu_custom_call" | custom-call | tf_op jit(solution)/shard_map/denoise_step/pallas_call | solution.py:428
  14.5 1.7 %multiply_add_fusion = (f32[2,12,8,128]{3,2,1,0:T(8,128)}, f32[2,12,8,128]{3,2,1,0:T(8,128)}) fusion(f32[2,12,8,128]{3,2,1,0:T(8,128)} %get-tuple-element.9, f32[2,12,8,128]{3,2,1,0:T(8,128)} %get-tuple-element.7, f32[2,12,8,128]{3,2,1,0:T(8,128)} %get-tuple-element.8, f32[12,8,128]{2,1,0:T(8,128)} %get-tuple-element.6), kind=kLoop, calls=%fused_computation | loop fusion | flops 73728 | bytes 540672 | tf_op jit(solution)/shard_map/add | solution.py:472
